TPU v7x, 32 devices: a whole 2x2x4 slice. The times are simulated.
32 devices in a mesh: band: 2 (over x), stn: 8 (over z, y), tm: 2 (over core).
Axes of the slice: x: 2, y: 2, z: 4, core: 2. Of those that a mesh axis runs over, the one named last changes fastest.
Arguments:
- voltages: int32 [704, 4, 32768], P('stn', 'band', 'tm'), parts along dimension 1, may hold values from -125 to 125, as said below
- filter_taps: float32 [16, 128], replicated, may hold values from -0.036 to 0.036
Outputs:
- visibilities: float32 [2, 2, 128, 704, 704], P(None, None, ('band', 'stn', 'tm')), parts along dimension 2
There are 2 independent parts, one for each index of `band`. A program takes and returns all parts, laid end to end along the dimension named above; an argument that names none is the same for every part. Nothing has to cross between parts.
Inputs may be any that keep to these rules, and one draw needn't show every extreme that they name: `voltages`: each input's samples are an integer gain of -2 to 2 times a signal common to all inputs plus noise of its own.
All inputs are finite; a program needn't handle non-finite values.
Results may differ from a plain program's by a relative error of at most 0.00049.
Values may be sent and summed in bfloat16 or wider, within the bound.
A program may use at most 192 MiB of HBM per device.

v0:
```python
import math
import jax
import jax.numpy as jnp
from jax import lax
from jax.sharding import PartitionSpec as P


def passed_along(value, axis, steps):
    count = lax.axis_size(axis)
    pairs = [(source, (source + steps) % count) for source in range(count)]
    return lax.ppermute(value, axis, pairs)


def transform_table(frame_len, chan_count):
    sample_index = jnp.arange(frame_len, dtype=jnp.int32)[:, None]
    chan_index = jnp.arange(chan_count, dtype=jnp.int32)[None, :]
    phase = (2 * chan_index + 1) * sample_index % (2 * frame_len)
    angle = phase.astype(jnp.float32) * (math.pi / frame_len)
    factor = 1.0 / math.sqrt(frame_len)
    cosine = jnp.cos(angle) * factor
    sine = -jnp.sin(angle) * factor
    return jnp.stack([cosine, sine], axis=2).reshape(frame_len, 2 * chan_count)


def arrange(blocks):
    stations, blocks_time, per_dev, parts_two, inputs_dev, sub_count, spec_dev = blocks.shape
    ordered = jnp.transpose(blocks, (3, 5, 2, 0, 4, 1, 6))
    return ordered.reshape(
        parts_two, sub_count, per_dev, stations * inputs_dev, blocks_time * spec_dev
    )


def correlate(stacked):
    real_in = stacked[0]
    imag_in = stacked[1]
    right_side = jnp.concatenate([real_in, imag_in], axis=-1)
    left_imag = jnp.concatenate([imag_in, -real_in], axis=-1)
    real_part = jnp.einsum(
        "gcis,gcjs->gcij", right_side, right_side, preferred_element_type=jnp.float32
    )
    imag_part = jnp.einsum(
        "gcis,gcjs->gcij", left_imag, right_side, preferred_element_type=jnp.float32
    )
    return jnp.stack([real_part, imag_part])


def shards(voltages, filter_taps):
    inputs_dev, sub_count, time_dev = voltages.shape
    taps_count, frame_len = filter_taps.shape
    spec_dev = time_dev // frame_len
    chan_count = frame_len // 2
    lagging = taps_count - 1
    frames = voltages.astype(jnp.bfloat16).reshape(inputs_dev, sub_count, spec_dev, frame_len)
    last_frames = frames[:, :, spec_dev - lagging :, :]
    received = passed_along(last_frames, "tm", 1)
    earlier = jnp.concatenate([jnp.zeros_like(received[:, :1]), received[:, :-1]], axis=1)
    history = jnp.where(lax.axis_index("tm") == 0, earlier, received)
    extended = jnp.concatenate([history, frames], axis=2).astype(jnp.float32)
    filtered = filter_taps[0] * extended[:, :, 0:spec_dev]
    for tap_index in range(1, taps_count):
        filtered = (
            filtered + filter_taps[tap_index] * extended[:, :, tap_index : tap_index + spec_dev]
        )
    table = transform_table(frame_len, chan_count)
    spectra = lax.dot_general(
        table,
        filtered.reshape(-1, frame_len),
        (((0,), (1,)), ((), ())),
        precision=lax.Precision.HIGHEST,
        preferred_element_type=jnp.float32,
    ).astype(jnp.bfloat16)
    stations = lax.axis_size("stn")
    halves = lax.axis_size("tm")
    scale = 1.0 / (spec_dev * halves)
    moved = lax.all_to_all(spectra[None], ("stn", "tm"), split_axis=1, concat_axis=0, tiled=True)
    per_dev = moved.shape[1] // 2
    blocks = moved.reshape(stations, halves, per_dev, 2, inputs_dev, sub_count, spec_dev)
    result = correlate(arrange(blocks))
    return result * scale


def solution(mesh):
    placed = (P("stn", "band", "tm"), P())
    return jax.shard_map(
        shards,
        mesh=mesh,
        in_specs=placed,
        out_specs=P(None, None, ("band", "stn", "tm"), None, None),
        check_vma=False,
    )
```

profile of v0, /device:TPU:1, one launch (start us, length us, event | category | flops | bytes accessed | tf_op | source)
XLA Modules:
  0.0 507.7 jit_solution(10586503539075918280)
XLA Ops:
  0.0 9.0 %convert_element_type.26 = bf16[88,2,16384]{2,1,0:T(2,128)(2,1)} convert(s32[88,2,16384]{2,1,0:T(2,128)} %param.2) | non-fusion elementwise | flops 2883584 | bytes 17301504 | tf_op jit(solution)/shard_map/convert_element_type | solution.py:53
  9.0 0.0 copy-start.1
  9.0 10.5 %reshape.154 = bf16[88,2,128,128]{3,2,1,0:T(8,128)(2,1)} reshape(bf16[88,2,16384]{2,1,0:T(2,128)(2,1)} %convert_element_type.26) | data formatting | bytes 11534336 | tf_op jit(solution)/shard_map/reshape | solution.py:53
  19.5 1.4 slice.146
  20.9 0.1 copy.33
  21.1 0.2 copy.19
  21.3 0.1 collective-permute-start
  21.4 0.2 cosine_multiply_fusion
  21.6 0.1 copy.17
  21.7 0.0 copy-done.1
  21.7 1.7 collective-permute-done
  23.5 0.1 copy.28
  23.6 0.2 pad_select_fusion
  23.7 10.6 %maximum_convert_fusion = f32[88,2,143,128]{3,2,0,1:T(8,128)} fusion(bf16[88,2,15,128]{3,2,0,1:T(8,128)(2,1)S(1)} %pad_select_fusion, bf16[88,2,128,128]{3,2,1,0:T(8,128)(2,1)} %reshape.154), kind=kLoop, calls=%fused_computation.36 | loop fusion | flops 12886016 | bytes 19329024 | tf_op jit(solution)/shard_map/convert_element_type | solution.py:58
  34.3 74.6 %fusion.1 = f32[88,2,128,128]{3,2,0,1:T(8,128)} fusion(f32[88,2,143,128]{3,2,0,1:T(8,128)} %maximum_convert_fusion, f32[128]{0:T(128)S(1)} %get-tuple-element.23, f32[128]{0:T(128)S(1)} %get-tuple-element.24, f32[128]{0:T(128)S(1)} %get-tuple-element.10, f32[128]{0:T(128)S(1)} %get-tuple-element.11, f32[128]{0:T(128)S(1)} %get-tuple-element.12, ...), kind=kLoop, calls=%fused_computation.4 | loop fusion | flops 89391104 | bytes 196091904 | tf_op jit(solution)/shard_map/add | solution.py:62
  109.0 10.6 %copy.22 = f32[88,2,128,128]{3,2,1,0:T(8,128)} copy(f32[88,2,128,128]{3,2,0,1:T(8,128)} %fusion.1) | data formatting | bytes 23068672 | tf_op jit(solution)/shard_map/add | solution.py:62
  119.6 13.6 %fusion = bf16[1,128,22528]{2,1,0:T(8,128)(2,1)S(1)} fusion(f32[128,128]{0,1:T(8,128)S(1)} %bitcast.54, f32[22528,128]{1,0:T(8,128)} %bitcast.52), kind=kOutput, calls=%fused_computation.2 | convolution fusion | flops 4432068608 | bytes 17367040 | tf_op jit(solution)/shard_map/dot_general | solution.py:65
  133.2 47.5 %copy.32 = bf16[1,128,22528]{2,0,1:T(2,128)(2,1)} copy(bf16[1,128,22528]{2,1,0:T(8,128)(2,1)S(1)} %fusion) | data formatting | bytes 11534336 | tf_op jit(solution)/shard_map/broadcast_in_dim | solution.py:75
  180.7 0.6 broadcast.142
  181.3 35.9 %reduce.2 = bf16[128,22528]{1,0:T(8,128)(2,1)} reduce(bf16[128,1,22528]{2,1,0:T(2,128)(2,1)} %bitcast.51, bf16[]{:T(256)} %broadcast.142), dimensions={1}, to_apply=%bitcast.50.reduce_sub_computation | reduce | bytes 11534338
  217.2 13.4 %reshape.156 = bf16[16,2,90112]{2,1,0:T(2,128)(2,1)} reshape(bf16[128,22528]{1,0:T(8,128)(2,1)} %reduce.2) | data formatting | bytes 11534336
  230.5 133.9 %all_to_all.4 = bf16[16,2,90112]{2,1,0:T(2,128)(2,1)} all-to-all(bf16[16,2,90112]{2,1,0:T(2,128)(2,1)} %reshape.156), channel_id=1, replica_groups=mesh['band'=2,'stn'=8,'tm'=2] {'stn','tm'}, dimensions={0} | all-to-all | bytes 11534336 | tf_op jit(solution)/shard_map/all_to_all | solution.py:75
  364.5 13.8 %reshape.157 = bf16[128,1,22528]{2,1,0:T(2,128)(2,1)} reshape(bf16[16,2,90112]{2,1,0:T(2,128)(2,1)} %all_to_all.4) | data formatting | bytes 11534336
  378.3 36.0 %bitcast_reduce_fusion = bf16[128,22528]{1,0:T(8,128)(2,1)} fusion(bf16[128,1,22528]{2,1,0:T(2,128)(2,1)} %reshape.157), kind=kLoop, calls=%fused_computation.75 | loop fusion | bytes 11534336 | tf_op jit(solution)/shard_map/all_to_all | solution.py:75
  414.3 8.9 %reshape.153 = bf16[8,2,4,2,88,2,128]{6,5,4,3,2,1,0:T(2,128)(2,1)} reshape(bf16[128,22528]{1,0:T(8,128)(2,1)} %bitcast_reduce_fusion) | data formatting | bytes 11534336 | tf_op jit(solution)/shard_map/reshape | solution.py:77
  423.2 8.4 %fusion.26 = (bf16[1,2,4,8,88,2,128]{6,1,4,0,2,5,3:T(2,128)(2,1)S(1)}, bf16[1,2,4,8,88,2,128]{6,1,4,0,2,5,3:T(2,128)(2,1)}) fusion(bf16[2,2,4,8,88,2,128]{6,1,4,0,2,5,3:T(2,128)(2,1)} %bitcast.53), kind=kLoop, calls=%fused_computation.73 | loop fusion | bytes 11534336 | tf_op jit(solution)/shard_map/slice | solution.py:35
  431.7 4.5 copy.25
  436.2 6.5 %squeeze.7 = bf16[2,4,704,256]{3,2,1,0:T(8,128)(2,1)S(1)} reshape(bf16[1,2,4,8,88,2,128]{6,5,4,3,2,1,0:T(2,128)(2,1)} %copy.25) | data formatting | bytes 5767168 | tf_op jit(solution)/shard_map/squeeze | solution.py:35
  442.8 6.4 %copy.24 = bf16[1,2,4,8,88,2,128]{6,5,4,3,2,1,0:T(2,128)(2,1)} copy(bf16[1,2,4,8,88,2,128]{6,1,4,0,2,5,3:T(2,128)(2,1)} %get-tuple-element.6) | data formatting | bytes 5767168 | tf_op jit(solution)/shard_map/slice | solution.py:34
  449.1 7.4 %squeeze.6 = bf16[2,4,704,256]{3,2,1,0:T(8,128)(2,1)} reshape(bf16[1,2,4,8,88,2,128]{6,5,4,3,2,1,0:T(2,128)(2,1)} %copy.24) | data formatting | bytes 5767168 | tf_op jit(solution)/shard_map/squeeze | solution.py:34
  456.6 5.0 fusion.27
  461.6 0.2 constant_dynamic-update-slice_fusion
  461.8 0.0 copy-start
  461.9 8.4 %convolution_bitcast_fusion.1 = f32[1,2,4,704,704]{4,3,2,1,0:T(8,128)} fusion(bf16[2,4,704,512]{3,2,1,0:T(8,128)(2,1)S(1)} %constant_dynamic-update-slice_fusion), kind=kOutput, calls=%fused_computation.35 | convolution fusion | flops 4060086272 | bytes 21626880 | tf_op jit(solution)/shard_map/gcis,gcjs->gcij/dot_general | solution.py:38
  470.3 0.0 copy-done
  470.3 14.1 %convolution_bitcast_fusion = f32[1,2,4,704,704]{4,3,2,1,0:T(8,128)} fusion(bf16[2,4,704,512]{3,2,1,0:T(8,128)(2,1)} %copy-done, bf16[2,4,704,256]{3,2,1,0:T(8,128)(2,1)} %get-tuple-element.7, bf16[2,4,704,256]{3,2,1,0:T(8,128)(2,1)S(1)} %squeeze.7), kind=kOutput, calls=%fused_computation.34 | convolution fusion | flops 4071620608 | bytes 27394048 | tf_op jit(solution)/shard_map/gcis,gcjs->gcij/dot_general | solution.py:41
  484.4 23.2 %maximum_multiply_fusion = f32[2,2,4,704,704]{4,3,2,1,0:T(8,128)} fusion(f32[1,2,4,704,704]{4,3,2,1,0:T(8,128)} %convolution_bitcast_fusion, f32[1,2,4,704,704]{4,3,2,1,0:T(8,128)} %convolution_bitcast_fusion.1), kind=kLoop, calls=%fused_computation | loop fusion | flops 15859712 | bytes 63438848 | tf_op jit(solution)/shard_map/mul | solution.py:79
  (4 shorter events, 0.0 us)
Async XLA Ops:
  9.0 12.7 %copy-start.1 = (f32[16,128]{1,0:T(8,128)S(1)}, f32[16,128]{1,0:T(8,128)}, u32[]{:S(2)}) copy-start(f32[16,128]{1,0:T(8,128)} %param.3) | copy-start | bytes 24580
  21.3 2.2 collective-permute-start
  461.8 8.4 %copy-start = (bf16[2,4,704,512]{3,2,1,0:T(8,128)(2,1)}, bf16[2,4,704,512]{3,2,1,0:T(8,128)(2,1)S(1)}, u32[]{:S(2)}) copy-start(bf16[2,4,704,512]{3,2,1,0:T(8,128)(2,1)S(1)} %constant_dynamic-update-slice_fusion) | copy-start | bytes 17301508
where the time goes:
time: 516 us; the launch traced here: 508 us
  local copies, waits for them, and re-layouts  177 us (34%)
  other arithmetic  159 us (31%)
  blocking collectives  134 us (26%)
  matrix products  36.1 us (7%)
    all_to_all x1, blocking collectives, shards(): lax.all_to_all(spectra[None], ('stn', 'tm'), split_axis=1, concat_axis=0,...  134 us
    add x1, other arithmetic, shards(): filtered + filter_taps[tap_index] * extended[:, :, tap_index:tap_index +...  74.6 us
    broadcast_in_dim x1, local copies, waits for them, and re-layouts, shards(): spectra[None]  47.5 us
    all_to_all x1, local copies, waits for them, and re-layouts, shards(): lax.all_to_all(spectra[None], ('stn', 'tm'), split_axis=1, concat_axis=0,...  36 us
    unnamed x1, other arithmetic  35.9 us
    unnamed x9, local copies, waits for them, and re-layouts  28 us
    mul x1, other arithmetic, shards(): return result * scale  23.2 us
    dot_general x1, matrix products, correlate(): jnp.einsum('gcis,gcjs->gcij', left_imag, right_side, preferred_element_ty...  14.1 us
  transfers between devices with their start and end apart: 1, of which 1 were waited for; matrix products, arithmetic and copies ran while one was open for 0% of the time, Pallas kernels for 0%

commit v1 on v0

--- a/solution.py
+++ b/solution.py
@@ -45,6 +45,18 @@
 
 
 def shards(voltages, filter_taps):
+
+    def run_shapes(mine_x):
+        return jnp.concatenate(
+            lax.all_to_all(
+                jnp.stack(jnp.split(mine_x, lax.psum(1, axis_name=("stn", "tm")), 1), 0),
+                ("stn", "tm"),
+                0,
+                0,
+            ),
+            axis=0,
+        )
+
     inputs_dev, sub_count, time_dev = voltages.shape
     taps_count, frame_len = filter_taps.shape
     spec_dev = time_dev // frame_len
@@ -72,7 +84,7 @@
     stations = lax.axis_size("stn")
     halves = lax.axis_size("tm")
     scale = 1.0 / (spec_dev * halves)
-    moved = lax.all_to_all(spectra[None], ("stn", "tm"), split_axis=1, concat_axis=0, tiled=True)
+    moved = run_shapes(spectra[None])
     per_dev = moved.shape[1] // 2
     blocks = moved.reshape(stations, halves, per_dev, 2, inputs_dev, sub_count, spec_dev)
     result = correlate(arrange(blocks))

time: 516 us -> 361 us (0.70); the launches traced: 508 us -> 360 us
  local copies, waits for them, and re-layouts: 177 us -> 66 us
  other arithmetic: 159 us -> 123 us
    broadcast_in_dim x1 -> x0, local copies, waits for them, and re-layouts: 47.5 us -> none  [shards(): spectra[None]]
    all_to_all x1 -> x0, local copies, waits for them, and re-layouts: 36 us -> none  [shards(): lax.all_to_all(spectra[None], ('stn', 'tm'), split_axis=1, concat_axis=0,...]
    unnamed x1 -> x0, other arithmetic: 35.9 us -> none
    unnamed x9 -> x21, local copies, waits for them, and re-layouts: 28 us -> 0.58 us
    another operation x0 -> x2, local copies, waits for them, and re-layouts: none -> 8.92 us  [the longest x1 8.89 us: shards(): moved.reshape(stations, halves, per_dev, 2, inputs_dev, sub_count, spec_dev)]
    reshape x1 -> x0, local copies, waits for them, and re-layouts: 8.89 us -> none  [shards(): moved.reshape(stations, halves, per_dev, 2, inputs_dev, sub_count, spec_dev)]
where the time goes in v1:
time: 361 us; the launch traced here: 360 us
  blocking collectives  134 us (37%)
  other arithmetic  123 us (34%)
  local copies, waits for them, and re-layouts  66 us (18%)
  matrix products  35.6 us (10%)
    all_to_all x1, blocking collectives, run_shapes(): lax.all_to_all(jnp.stack(jnp.split(mine_x, lax.psum(1, axis_name=('stn',...  134 us
    add x1, other arithmetic, shards(): filtered + filter_taps[tap_index] * extended[:, :, tap_index:tap_index +...  74.6 us
    mul x1, other arithmetic, shards(): return result * scale  23.2 us
    dot_general x1, matrix products, correlate(): jnp.einsum('gcis,gcjs->gcij', left_imag, right_side, preferred_element_ty...  14.1 us
    dot_general x1, matrix products, shards(): lax.dot_general(table, filtered.reshape(-1, frame_len), (((0,), (1,)), ((...  13.1 us
    slice x2, local copies, waits for them, and re-layouts, correlate(): imag_in = stacked[1]  13 us
    add x1, local copies, waits for them, and re-layouts, shards(): filtered + filter_taps[tap_index] * extended[:, :, tap_index:tap_index +...  10.6 us
    convert_element_type x1, other arithmetic, shards(): extended = jnp.concatenate([history, frames], axis=2).astype(jnp.float32)  10.6 us
  transfers between devices with their start and end apart: 1, of which 1 were waited for; matrix products, arithmetic and copies ran while one was open for 0% of the time, Pallas kernels for 0%

profile of v1, /device:TPU:1, one launch (start us, length us, event | category | flops | bytes accessed | tf_op | source)
XLA Modules:
  0.0 360.1 jit_solution(6691284587719321015)
XLA Ops:
  0.0 9.0 %convert_element_type.26 = bf16[88,2,16384]{2,1,0:T(2,128)(2,1)} convert(s32[88,2,16384]{2,1,0:T(2,128)} %param.2) | non-fusion elementwise | flops 2883584 | bytes 17301504 | tf_op jit(solution)/shard_map/convert_element_type | solution.py:65
  9.0 0.0 copy-start.1
  9.0 10.5 %reshape.146 = bf16[88,2,128,128]{3,2,1,0:T(8,128)(2,1)} reshape(bf16[88,2,16384]{2,1,0:T(2,128)(2,1)} %convert_element_type.26) | data formatting | bytes 11534336 | tf_op jit(solution)/shard_map/reshape | solution.py:65
  19.5 1.4 slice.146
  20.9 0.1 copy.29
  21.1 0.2 copy.18
  21.3 0.1 collective-permute-start
  21.4 0.2 cosine_multiply_fusion
  21.6 0.1 copy.16
  21.7 0.0 copy-done.1
  21.7 1.7 collective-permute-done
  23.5 0.1 copy.26
  23.5 0.2 pad_select_fusion
  23.7 10.6 %maximum_convert_fusion = f32[88,2,143,128]{3,2,0,1:T(8,128)} fusion(bf16[88,2,15,128]{3,2,0,1:T(8,128)(2,1)S(1)} %pad_select_fusion, bf16[88,2,128,128]{3,2,1,0:T(8,128)(2,1)} %reshape.146), kind=kLoop, calls=%fused_computation.36 | loop fusion | flops 12886016 | bytes 19329024 | tf_op jit(solution)/shard_map/convert_element_type | solution.py:70
  34.3 74.6 %fusion.1 = f32[88,2,128,128]{3,2,0,1:T(8,128)} fusion(f32[88,2,143,128]{3,2,0,1:T(8,128)} %maximum_convert_fusion, f32[128]{0:T(128)S(1)} %get-tuple-element.23, f32[128]{0:T(128)S(1)} %get-tuple-element.24, f32[128]{0:T(128)S(1)} %get-tuple-element.10, f32[128]{0:T(128)S(1)} %get-tuple-element.11, f32[128]{0:T(128)S(1)} %get-tuple-element.12, ...), kind=kLoop, calls=%fused_computation.4 | loop fusion | flops 89391104 | bytes 196091904 | tf_op jit(solution)/shard_map/add | solution.py:74
  108.9 10.6 %copy.21 = f32[88,2,128,128]{3,2,1,0:T(8,128)} copy(f32[88,2,128,128]{3,2,0,1:T(8,128)} %fusion.1) | data formatting | bytes 23068672 | tf_op jit(solution)/shard_map/add | solution.py:74
  119.6 13.1 %fusion = bf16[1,128,22528]{2,1,0:T(8,128)(2,1)S(1)} fusion(f32[128,128]{0,1:T(8,128)S(1)} %bitcast.114, f32[22528,128]{1,0:T(8,128)} %bitcast.112), kind=kOutput, calls=%fused_computation.2 | convolution fusion | flops 4432068608 | bytes 17367040 | tf_op jit(solution)/shard_map/dot_general | solution.py:77
  133.2 133.6 %all_to_all.5 = bf16[16,1,8,22528]{3,2,1,0:T(8,128)(2,1)} all-to-all(bf16[16,1,8,22528]{3,2,1,0:T(8,128)(2,1)S(1)} %fusion.19), channel_id=1, replica_groups=mesh['band'=2,'stn'=8,'tm'=2] {'stn','tm'}, dimensions={0} | all-to-all | bytes 11534336 | tf_op jit(solution)/shard_map/all_to_all | solution.py:51
  266.8 8.9 %reshape_reshape.3 = bf16[8,2,4,2,88,2,128]{6,5,4,3,2,1,0:T(2,128)(2,1)} reshape(bf16[16,1,8,22528]{3,2,1,0:T(8,128)(2,1)} %all_to_all.5) | data formatting | bytes 11534336 | tf_op jit(solution)/shard_map/reshape;reshape | solution.py:89
  275.7 8.5 %fusion.42 = (bf16[1,2,4,8,88,2,128]{6,1,4,0,2,5,3:T(2,128)(2,1)S(1)}, bf16[1,2,4,8,88,2,128]{6,1,4,0,2,5,3:T(2,128)(2,1)}) fusion(bf16[2,2,4,8,88,2,128]{6,1,4,0,2,5,3:T(2,128)(2,1)} %bitcast.113), kind=kLoop, calls=%fused_computation.105 | loop fusion | bytes 11534336 | tf_op jit(solution)/shard_map/slice | solution.py:35
  284.2 4.5 %copy.23 = bf16[1,2,4,8,88,2,128]{6,5,4,3,2,1,0:T(2,128)(2,1)} copy(bf16[1,2,4,8,88,2,128]{6,1,4,0,2,5,3:T(2,128)(2,1)S(1)} %get-tuple-element.5) | data formatting | bytes 5767168 | tf_op jit(solution)/shard_map/slice | solution.py:35
  288.7 6.6 %squeeze.7 = bf16[2,4,704,256]{3,2,1,0:T(8,128)(2,1)S(1)} reshape(bf16[1,2,4,8,88,2,128]{6,5,4,3,2,1,0:T(2,128)(2,1)} %copy.23) | data formatting | bytes 5767168 | tf_op jit(solution)/shard_map/squeeze | solution.py:35
  295.3 6.4 %copy.22 = bf16[1,2,4,8,88,2,128]{6,5,4,3,2,1,0:T(2,128)(2,1)} copy(bf16[1,2,4,8,88,2,128]{6,1,4,0,2,5,3:T(2,128)(2,1)} %get-tuple-element.6) | data formatting | bytes 5767168 | tf_op jit(solution)/shard_map/slice | solution.py:34
  301.7 7.4 %squeeze.6 = bf16[2,4,704,256]{3,2,1,0:T(8,128)(2,1)} reshape(bf16[1,2,4,8,88,2,128]{6,5,4,3,2,1,0:T(2,128)(2,1)} %copy.22) | data formatting | bytes 5767168 | tf_op jit(solution)/shard_map/squeeze | solution.py:34
  309.1 5.0 %fusion.43 = (bf16[2,4,704,256]{3,2,1,0:T(8,128)(2,1)}, bf16[2,4,704,512]{3,2,1,0:T(8,128)(2,1)S(1)}) fusion(bf16[2,4,704,256]{3,2,1,0:T(8,128)(2,1)} %squeeze.6), kind=kLoop, calls=%fused_computation.106 | loop fusion | flops 4325375 | bytes 8650752 | tf_op jit(solution)/shard_map/neg | solution.py:37
  314.2 0.2 constant_dynamic-update-slice_fusion
  314.4 0.0 copy-start
  314.4 8.4 %convolution_bitcast_fusion.1 = f32[1,2,4,704,704]{4,3,2,1,0:T(8,128)} fusion(bf16[2,4,704,512]{3,2,1,0:T(8,128)(2,1)S(1)} %constant_dynamic-update-slice_fusion), kind=kOutput, calls=%fused_computation.35 | convolution fusion | flops 4060086272 | bytes 21626880 | tf_op jit(solution)/shard_map/gcis,gcjs->gcij/dot_general | solution.py:38
  322.8 0.0 copy-done
  322.8 14.1 %convolution_bitcast_fusion = f32[1,2,4,704,704]{4,3,2,1,0:T(8,128)} fusion(bf16[2,4,704,512]{3,2,1,0:T(8,128)(2,1)} %copy-done, bf16[2,4,704,256]{3,2,1,0:T(8,128)(2,1)} %get-tuple-element.7, bf16[2,4,704,256]{3,2,1,0:T(8,128)(2,1)S(1)} %squeeze.7), kind=kOutput, calls=%fused_computation.34 | convolution fusion | flops 4071620608 | bytes 27394048 | tf_op jit(solution)/shard_map/gcis,gcjs->gcij/dot_general | solution.py:41
  336.9 23.2 %maximum_multiply_fusion = f32[2,2,4,704,704]{4,3,2,1,0:T(8,128)} fusion(f32[1,2,4,704,704]{4,3,2,1,0:T(8,128)} %convolution_bitcast_fusion, f32[1,2,4,704,704]{4,3,2,1,0:T(8,128)} %convolution_bitcast_fusion.1), kind=kLoop, calls=%fused_computation | loop fusion | flops 15859712 | bytes 63438848 | tf_op jit(solution)/shard_map/mul | solution.py:91
  (20 shorter events, 0.5 us)
Async XLA Ops:
  9.0 12.7 %copy-start.1 = (f32[16,128]{1,0:T(8,128)S(1)}, f32[16,128]{1,0:T(8,128)}, u32[]{:S(2)}) copy-start(f32[16,128]{1,0:T(8,128)} %param.3) | copy-start | bytes 24580
  21.3 2.2 collective-permute-start
  314.4 8.4 %copy-start = (bf16[2,4,704,512]{3,2,1,0:T(8,128)(2,1)}, bf16[2,4,704,512]{3,2,1,0:T(8,128)(2,1)S(1)}, u32[]{:S(2)}) copy-start(bf16[2,4,704,512]{3,2,1,0:T(8,128)(2,1)S(1)} %constant_dynamic-update-slice_fusion) | copy-start | bytes 17301508
